TPU v7x, 32 devices: a whole 2x2x4 slice. The times are simulated.
32 devices in a mesh: head: 4 (over z), ctx: 8 (over y, x, core).
Axes of the slice: x: 2, y: 2, z: 4, core: 2. Of those that a mesh axis runs over, the one named last changes fastest.
Arguments:
- query_input: bfloat16 [4, 16, 1536], P(None, 'ctx'), may hold values from -6 to 6
- new_latent: bfloat16 [4, 16, 512], P(None, 'ctx'), may hold values from -30 to 30
- new_rotary: bfloat16 [4, 16, 64], P(None, 'ctx'), may hold values from -6 to 6
- lengths: int32 [16], replicated, may hold values from 1 to 16384, as said below
- adapter_index: int32 [2], replicated, may hold values from 0 to 7
- query_up: bfloat16 [1536, 128, 192], P('ctx', 'head'), may hold values from -0.15625 to 0.15625
- latent_up: bfloat16 [512, 128, 256], P('ctx', 'head'), may hold values from -0.25 to 0.25
- query_adapter_down: bfloat16 [8, 1536, 64], replicated, may hold values from -0.15625 to 0.15625
- query_adapter_up: bfloat16 [8, 64, 128, 192], P(None, None, 'head'), may hold values from -0.75 to 0.75
- latent_adapter_down: bfloat16 [8, 512, 64], replicated, may hold values from -0.25 to 0.25
- latent_adapter_up: bfloat16 [8, 64, 128, 256], P(None, None, 'head'), may hold values from -0.75 to 0.75
- cache_latent: bfloat16 [16384, 512], P('ctx'), may hold values from -20 to 20
- cache_rotary: bfloat16 [64, 16384], P(None, 'ctx'), may hold values from -1200 to 1200
- output_weight: bfloat16 [16384, 7168], P('head', 'ctx'), may hold values from -0.046875 to 0.046875
Outputs:
- attention_output: bfloat16 [4, 16, 7168], P(None, 'head', 'ctx')
Inputs may be any that keep to these rules, and one draw needn't show every extreme that they name: Row r attends to cached positions 0 to lengths[r] - 1; some row's length is exactly 16384.
All inputs are finite; a program needn't handle non-finite values.
Results may differ from a plain program's by a relative error of at most 0.012.
The roundings to bfloat16 on the way count: a program that leaves them out, or rounds other values in their place, can miss the bound.
Values may be sent and summed in bfloat16 or wider, within the bound.
A program may use at most 256 MiB of HBM per device.

v0:
```python
import math

import jax
import jax.numpy as jnp
from jax import lax
from jax.sharding import PartitionSpec as P

LATENT = 512
NOPE_DIM = 128
ROTARY = 64


NEG = -1e30


def joined(value, axis, join):
    pieces = jax.tree.map(lambda part: lax.all_gather(part, axis), value)
    head = jax.tree.map(lambda part: part[0], pieces)
    tail = jax.tree.map(lambda part: part[1:], pieces)
    subtotal, _ = lax.scan(lambda subtotal, piece: (join(subtotal, piece), None), head, tail)
    return subtotal


def rotate(raw, positions):
    half = raw.shape[-1] // 2
    freq = jnp.exp(jnp.arange(half, dtype=jnp.float32) * (-math.log(10000.0) / half))
    angle = positions[..., None] * freq
    cosine = jnp.cos(angle)
    sine = jnp.sin(angle)
    first = raw[..., :half]
    second = raw[..., half:]
    return jnp.concatenate(
        [first * cosine - second * sine, second * cosine + first * sine], axis=-1
    )


def combine_states(first, second):
    top_first, total_first, mixed_first = first
    top_second, total_second, mixed_second = second
    top = jnp.maximum(top_first, top_second)
    factor_first = jnp.exp(top_first - top)
    factor_second = jnp.exp(top_second - top)
    total = total_first * factor_first + total_second * factor_second
    mixed = mixed_first * factor_first[..., None] + mixed_second * factor_second[..., None]
    return (top, total, mixed)


def value_project(states, value_wide):
    return jnp.einsum(
        "srhk,khv->srhv",
        states,
        value_wide,
        precision=lax.Precision.HIGHEST,
        preferred_element_type=jnp.float32,
    )


def on_device(
    query_input,
    new_latent,
    new_rotary,
    lengths,
    adapter_index,
    query_up,
    latent_up,
    query_adapter_down,
    query_adapter_up,
    latent_adapter_down,
    latent_adapter_up,
    cache_latent,
    cache_rotary,
    output_weight,
):
    chosen_query = adapter_index[0]
    chosen_latent = adapter_index[1]
    down_query = lax.dynamic_index_in_dim(query_adapter_down, chosen_query, 0, keepdims=False)
    upper_query = lax.dynamic_index_in_dim(query_adapter_up, chosen_query, 0, keepdims=False)
    down_latent = lax.dynamic_index_in_dim(latent_adapter_down, chosen_latent, 0, keepdims=False)
    upper_latent = lax.dynamic_index_in_dim(latent_adapter_up, chosen_latent, 0, keepdims=False)
    latent_full = lax.all_gather(latent_up, "ctx", axis=0, tiled=True)
    latent_merged = (
        latent_full.astype(jnp.float32)
        + jnp.einsum("kr,rhd->khd", down_latent, upper_latent, preferred_element_type=jnp.float32)
    ).astype(jnp.bfloat16)
    key_weight = latent_merged[:, :, :NOPE_DIM]
    value_wide = latent_merged[:, :, NOPE_DIM:].astype(jnp.float32)
    merged = (
        lax.all_gather(query_up, "ctx", axis=0, tiled=True).astype(jnp.float32)
        + jnp.einsum("nr,rhd->nhd", down_query, upper_query, preferred_element_type=jnp.float32)
    ).astype(jnp.bfloat16)
    folded = jnp.einsum(
        "nhd,khd->nhk", merged[:, :, :NOPE_DIM], key_weight, preferred_element_type=jnp.float32
    ).astype(jnp.bfloat16)
    query_map = jnp.concatenate([folded, merged[:, :, NOPE_DIM:]], axis=2)
    step_count = query_input.shape[0]
    row_count = query_input.shape[1]
    row_start = lax.axis_index("ctx") * row_count
    local_lengths = lax.dynamic_slice_in_dim(lengths, row_start, row_count, 0)
    product = jnp.einsum(
        "srq,qhe->srhe", query_input, query_map, preferred_element_type=jnp.float32
    )
    project_step_count = query_input.shape[0]
    positions = (
        local_lengths[None, :] + jnp.arange(project_step_count, dtype=jnp.int32)[:, None]
    ).astype(jnp.float32)[:, :, None]
    latent_part = product[..., :LATENT].astype(jnp.bfloat16)
    rotary_part = rotate(product[..., LATENT:], positions).astype(jnp.bfloat16)
    query_latent, query_rotary = (
        lax.all_gather(latent_part, "ctx", axis=1, tiled=True),
        lax.all_gather(rotary_part, "ctx", axis=1, tiled=True),
    )
    span = cache_latent.shape[0]
    offset = lax.axis_index("ctx") * span
    visible = (offset + jnp.arange(span, dtype=jnp.int32))[None, :] < lengths[:, None]
    scale = 1.0 / math.sqrt(NOPE_DIM + ROTARY)
    tops = []
    totals = []
    mixes = []
    for step in range(step_count):
        scores = jnp.einsum(
            "rhk,tk->rht", query_latent[step], cache_latent, preferred_element_type=jnp.float32
        )
        scores = scores + jnp.einsum(
            "rhe,et->rht", query_rotary[step], cache_rotary, preferred_element_type=jnp.float32
        )
        scores = jnp.where(visible[:, None, :], scores * scale, NEG)
        top = jnp.max(scores, axis=2)
        weight = jnp.where(visible[:, None, :], jnp.exp(scores - top[..., None]), 0.0)
        tops.append(top)
        totals.append(jnp.sum(weight, axis=2))
        mixes.append(
            jnp.einsum(
                "rht,tk->rhk",
                weight.astype(jnp.bfloat16),
                cache_latent,
                preferred_element_type=jnp.float32,
            )
        )
    top_part = jnp.stack(tops)
    total_part = jnp.stack(totals)
    mixed_part = jnp.stack(mixes)
    top_all, total_all, mixed_all = joined(
        (top_part, total_part, mixed_part), "ctx", combine_states
    )
    top_local = lax.dynamic_slice_in_dim(top_all, row_start, row_count, 1)
    total_local = lax.dynamic_slice_in_dim(total_all, row_start, row_count, 1)
    mixed_local = lax.dynamic_slice_in_dim(mixed_all, row_start, row_count, 1)
    own = jnp.einsum("srhk,jrk->srhj", latent_part, new_latent, preferred_element_type=jnp.float32)
    own = own + jnp.einsum(
        "srhe,jre->srhj", rotary_part, new_rotary, preferred_element_type=jnp.float32
    )
    causal = (
        jnp.arange(step_count, dtype=jnp.int32)[None, :]
        <= jnp.arange(step_count, dtype=jnp.int32)[:, None]
    )[:, None, None, :]
    own = jnp.where(causal, own * scale, NEG)
    top_final = jnp.maximum(top_local, jnp.max(own, axis=3))
    carried = jnp.exp(top_local - top_final)
    own_weight = jnp.where(causal, jnp.exp(own - top_final[..., None]), 0.0)
    total = total_local * carried + jnp.sum(own_weight, axis=3)
    own_mixed = jnp.einsum(
        "srhj,jrk->srhk",
        own_weight.astype(jnp.bfloat16),
        new_latent,
        preferred_element_type=jnp.float32,
    )
    attended = (mixed_local * carried[..., None] + own_mixed) / total[..., None]
    head_value = value_project(attended, value_wide)
    head_output = head_value.astype(jnp.bfloat16)
    head_flat = head_output.reshape(
        step_count, row_count, head_output.shape[2] * head_output.shape[3]
    )
    partial_out = jnp.einsum(
        "srf,fd->srd",
        lax.all_gather(head_flat, "ctx", axis=1, tiled=True),
        output_weight,
        preferred_element_type=jnp.float32,
    )
    return lax.psum_scatter(
        partial_out.astype(jnp.bfloat16), "head", scatter_dimension=1, tiled=True
    )


def solution(mesh):
    placed = (
        P(None, "ctx", None),
        P(None, "ctx", None),
        P(None, "ctx", None),
        P(),
        P(),
        P("ctx", "head", None),
        P("ctx", "head", None),
        P(),
        P(None, None, "head", None),
        P(),
        P(None, None, "head", None),
        P("ctx", None),
        P(None, "ctx"),
        P("head", "ctx"),
    )
    return jax.shard_map(
        on_device, mesh=mesh, in_specs=placed, out_specs=P(None, "head", "ctx"), check_vma=False
    )
```

profile of v0, /device:TPU:0, one launch (start us, length us, event | category | flops | bytes accessed | tf_op | source)
XLA Modules:
  0.0 642.3 jit_solution(15251347217707779111)
XLA Ops:
  6.5 3.0 copy.54
  9.6 0.7 all-gather.10.cloned.1.call-update
  10.3 0.6 fusion.132
  14.8 2.3 constant_dynamic-slice_fusion.1
  17.1 1.3 constant_dynamic-slice_fusion
  18.4 48.4 %all-gather.8.cloned.1.call-done = bf16[512,32,256]{2,0,1:T(8,128)(2,1)} async-done(((bf16[64,32,256]{2,0,1:T(8,128)(2,1)}), bf16[512,32,256]{2,0,1:T(8,128)(2,1)}) %all-gather.8.cloned.1.call-update) | async-done | bytes 8388624 | tf_op jit(solution)/shard_map/all_gather | solution.py:80
  66.8 10.1 %add_convert_fusion.1 = bf16[512,32,256]{2,0,1:T(8,128)(2,1)} fusion(bf16[512,32,256]{2,0,1:T(8,128)(2,1)} %all-gather.8.cloned.1.call-done, bf16[1,64,32,256]{3,2,1,0:T(8,128)(2,1)} %constant_dynamic-slice_fusion.1, bf16[8,512,64]{1,2,0:T(8,128)(2,1)} %param.25, s32[]{:T(128)S(6)} %select_n.53), kind=kOutput, calls=%fused_computation.12 | convolution fusion | flops 549453824 | bytes 17891332 | tf_op jit(solution)/shard_map/kr,rhd->khd/dot_general | solution.py:83
  76.9 117.2 %all-gather.10.cloned.1.call-done = bf16[1536,32,192]{2,1,0:T(8,128)(2,1)} async-done(((bf16[192,32,192]{2,1,0:T(8,128)(2,1)}), bf16[1536,32,192]{2,1,0:T(8,128)(2,1)}) %all-gather.10.cloned.1.call-update) | async-done | bytes 18874384 | tf_op jit(solution)/shard_map/all_gather | solution.py:88
  194.0 31.0 %copy.56 = bf16[1536,32,192]{0,2,1:T(8,128)(2,1)} copy(bf16[1536,32,192]{2,1,0:T(8,128)(2,1)} %all-gather.10.cloned.1.call-done) | data formatting | bytes 37748736 | tf_op jit(solution)/shard_map/all_gather | solution.py:88
  225.0 13.7 %add_convert_fusion = bf16[1536,32,192]{0,2,1:T(8,128)(2,1)} fusion(bf16[1536,32,192]{0,2,1:T(8,128)(2,1)} %copy.56, bf16[1,64,32,192]{3,2,1,0:T(8,128)(2,1)S(1)} %constant_dynamic-slice_fusion, bf16[8,1536,64]{1,2,0:T(8,128)(2,1)} %param.23, s32[]{:T(128)S(6)} %select_n.54), kind=kOutput, calls=%fused_computation.11 | convolution fusion | flops 1236271104 | bytes 38731780 | tf_op jit(solution)/shard_map/nr,rhd->nhd/dot_general | solution.py:89
  238.7 6.1 slice.105
  244.8 24.9 %convert_bitcast_fusion = bf16[1536,32,512]{0,2,1:T(8,128)(2,1)} fusion(bf16[1536,32,192]{0,2,1:T(8,128)(2,1)} %add_convert_fusion, bf16[512,32,256]{2,0,1:T(8,128)(2,1)} %add_convert_fusion.1), kind=kOutput, calls=%fused_computation.10 | convolution fusion | flops 6467616768 | bytes 67108864 | tf_op jit(solution)/shard_map/nhd,khd->nhk/dot_general | solution.py:91
  269.8 26.8 %fusion.69 = f32[4,2,32,576]{3,0,1,2:T(4,128)S(1)} fusion(bf16[1536,32,64]{0,2,1:T(8,128)(2,1)} %slice.105, bf16[1536,32,512]{0,2,1:T(8,128)(2,1)} %convert_bitcast_fusion, bf16[4,2,1536]{2,1,0:T(2,128)(2,1)S(1)} %copy-done.10), kind=kOutput, calls=%fused_computation.68 | convolution fusion | flops 566231040 | bytes 57237504 | tf_op jit(solution)/shard_map/srq,qhe->srhe/dot_general | solution.py:99
  296.6 0.8 slice.138
  297.4 0.0 all-gather.14.cloned.1.call-start
  297.5 0.1 dynamic_slice.43
  297.6 0.1 add_convert_fusion.3
  297.7 0.1 multiply_cosine_fusion
  297.8 0.1 broadcast_compare_fusion
  297.9 0.1 subtract_convert_fusion
  298.0 0.1 pad_maximum_fusion.1
  298.2 10.4 %all_gather.36 = bf16[4,16,32,64]{3,0,1,2:T(4,128)(2,1)S(1)} all-gather(bf16[4,2,32,64]{3,0,1,2:T(4,128)(2,1)S(1)} %pad_maximum_fusion.1), channel_id=1, replica_groups=mesh['head'=4,'ctx'=8] {'ctx'}, dimensions={1}, use_global_device_ids=true | all-gather | bytes 294912 | tf_op jit(solution)/shard_map/all_gather | solution.py:110
  308.5 0.8 fusion.131
  309.3 16.5 %all-gather.12.cloned.1.call-done = bf16[4,16,32,512]{3,0,1,2:T(4,128)(2,1)} async-done(((bf16[4,2,32,512]{3,0,1,2:T(4,128)(2,1)}), bf16[4,16,32,512]{3,0,1,2:T(4,128)(2,1)}) %all-gather.12.cloned.1.call-update) | async-done | bytes 2097168 | tf_op jit(solution)/shard_map/all_gather | solution.py:109
  325.8 8.1 %fusion.130 = (bf16[1,16,32,512]{3,0,1,2:T(2,128)(2,1)S(1)}, bf16[1,16,32,512]{3,0,1,2:T(2,128)(2,1)S(1)}, bf16[1,16,32,512]{3,0,1,2:T(2,128)(2,1)S(1)}, bf16[1,16,32,512]{3,0,1,2:T(2,128)(2,1)S(1)}) fusion(bf16[4,16,32,512]{3,0,1,2:T(4,128)(2,1)} %all-gather.12.cloned.1.call-done), kind=kLoop, calls=%fused_computation.149 | loop fusion | bytes 4194304 | tf_op jit(solution)/shard_map/slice | solution.py:121
  333.9 1.6 fusion.29
  335.5 1.6 fusion.31
  337.1 1.6 fusion.33
  338.7 1.6 fusion.35
  340.3 1.1 fusion.133
  341.5 1.1 fusion.134
  342.6 1.1 fusion.135
  343.7 1.1 fusion.136
  344.8 1.3 fusion.64
  346.1 1.3 fusion.59
  347.4 1.5 fusion.54
  349.0 1.3 fusion.49
  350.3 2.5 pad_maximum_fusion
  352.8 0.0 all-reduce.3.cloned.1.call-start
  352.9 0.9 copy-done.7
  353.7 0.3 fusion.98
  354.0 0.2 fusion.137
  354.3 9.3 %all-gather = f32[32,16,32]{2,1,0:T(8,128)S(1)} all-gather(f32[4,16,32]{2,1,0:T(8,128)S(1)} %pad_maximum_fusion.2), channel_id=2, replica_groups=mesh['head'=4,'ctx'=8] {'ctx'}, dimensions={0}, use_global_device_ids=true | all-gather | bytes 73728 | tf_op jit(solution)/shard_map/all_gather | solution.py:17
  363.5 9.6 %fusion.10 = (f32[16,32]{1,0:T(8,128)S(1)}, f32[16,32]{1,0:T(8,128)S(1)}, f32[16,32]{1,0:T(8,128)S(1)}, f32[16,32]{1,0:T(8,128)S(1)}) fusion(f32[16,32,2048]{2,1,0:T(8,128)} %copy-done.4, f32[16,32]{1,0:T(8,128)S(1)} %get-tuple-element.93, pred[16,2048]{1,0:T(8,128)(4,1)S(1)} %broadcast_compare_fusion, f32[16,32,2048]{2,1,0:T(8,128)} %copy-done.3, ...), kind=kLoop, calls=%fused_computation.29 | loop fusion | flops 12580864 | bytes 16826368 | tf_op jit(solution)/shard_map/reduce_sum | solution.py:130
  373.2 9.8 %all-gather.1 = f32[32,16,32]{2,1,0:T(8,128)S(1)} all-gather(f32[4,16,32]{2,1,0:T(8,128)S(1)} %pad_maximum_fusion.3), channel_id=3, replica_groups=mesh['head'=4,'ctx'=8] {'ctx'}, dimensions={0}, use_global_device_ids=true | all-gather | bytes 73728 | tf_op jit(solution)/shard_map/all_gather | solution.py:17
  383.1 131.8 %all-gather.14.cloned.1.call-done = f32[32,16,32,512]{3,2,1,0:T(8,128)} async-done(((f32[4,16,32,512]{3,2,1,0:T(8,128)}), f32[32,16,32,512]{3,2,1,0:T(8,128)}) %all-gather.14.cloned.1.call-update) | async-done | bytes 33554448 | tf_op jit(solution)/shard_map/all_gather | solution.py:17
  514.8 4.9 slice.119
  519.8 22.8 %slice.122 = f32[28,16,32,512]{3,2,1,0:T(8,128)} slice(f32[32,16,32,512]{3,2,1,0:T(8,128)} %all-gather.14.cloned.1.call-done), slice={[4:32], [0:16], [0:32], [0:512]} | slice | bytes 58720256 | tf_op jit(solution)/shard_map/slice | solution.py:19
  542.6 36.5 %while.14 = (s32[]{:T(128)}, f32[4,16,32]{2,1,0:T(8,128)S(1)}, f32[4,16,32]{2,1,0:T(8,128)S(1)}, f32[4,16,32,512]{3,2,1,0:T(8,128)}, f32[7,4,16,32]{3,2,1,0:T(8,...) while((s32[]{:T(128)}, f32[4,16,32]{2,1,0:T(8,128)S(1)}, ...), condition=%wide.region_9.10_spmd, body=%wide.region_8.9_spmd.sunk | while | flops 3158018 | bytes 12664933 | solution.py:20
  542.6 5.2 fusion.147
  547.8 5.2 fusion.147
  553.0 5.2 fusion.147
  558.2 5.2 fusion.147
  563.4 5.2 fusion.147
  568.6 5.2 fusion.147
  573.8 5.2 fusion.147
  579.1 0.1 fusion.116
  579.2 1.3 fusion.71
  580.6 4.2 fusion.76
  584.8 9.8 %all_gather.43 = bf16[4,16,4096]{2,0,1:T(4,128)(2,1)S(1)} all-gather(bf16[4,2,4096]{2,0,1:T(4,128)(2,1)S(1)} %bitcast.183), channel_id=1, replica_groups=mesh['head'=4,'ctx'=8] {'ctx'}, dimensions={1}, use_global_device_ids=true | all-gather | bytes 589824 | tf_op jit(solution)/shard_map/all_gather | solution.py:175
  594.6 5.3 fusion.72
  599.9 0.6 dynamic-slice
  601.2 33.0 %all-reduce.3.cloned.1.call-done = bf16[4,16,896]{2,1,0:T(8,128)(2,1)} async-done(((bf16[4,16,896]{2,1,0:T(8,128)(2,1)}), bf16[4,16,896]{2,1,0:T(8,128)(2,1)}) %all-reduce.3.cloned.1.call-update) | async-done | bytes 114704
  634.2 1.4 constant_dynamic-slice_fusion.2
  (58 shorter events, 0.5 us)
Async XLA Ops:
  6.5 327.3 %copy-start = (bf16[2048,512]{1,0:T(8,128)(2,1)S(1)}, bf16[2048,512]{1,0:T(8,128)(2,1)}, u32[]{:S(2)}) copy-start(bf16[2048,512]{1,0:T(8,128)(2,1)} %param.27) | copy-start | bytes 6291460
  6.5 3.8 copy-start.8
  6.5 60.2 %all-gather.8.cloned.1.call-start = ((), (), s32[]{:S(2)}) async-start(), calls=%async_computation | async-start | bytes 9437184 | tf_op jit(solution)/shard_map/all_gather | solution.py:80
  9.5 184.5 %all-gather.10.cloned.1.call-start = ((), (), s32[]{:S(2)}) async-start(), calls=%async_computation.1 | async-start | bytes 28311552 | tf_op jit(solution)/shard_map/all_gather | solution.py:88
  10.3 315.5 %all-gather.12.cloned.1.call-start = ((), (), s32[]{:S(2)}) async-start(), calls=%async_computation.2 | async-start | bytes 2359296 | tf_op jit(solution)/shard_map/all_gather | solution.py:109
  244.8 25.0 %copy-start.10 = (bf16[4,2,1536]{2,1,0:T(2,128)(2,1)S(1)}, bf16[4,2,1536]{2,1,0:T(2,128)(2,1)}, u32[]{:S(2)}) copy-start(bf16[4,2,1536]{2,1,0:T(2,128)(2,1)} %param.16) | copy-start | bytes 73732
  269.8 27.7 %copy-start.9 = (s32[16]{0:T(128)S(1)}, s32[16]{0:T(128)}, u32[]{:S(2)}) copy-start(s32[16]{0:T(128)} %param.19) | copy-start | bytes 196
  297.4 217.4 %all-gather.14.cloned.1.call-start = ((), (), s32[]{:S(2)}) async-start(), calls=%async_computation.3 | async-start | bytes 37748736 | tf_op jit(solution)/shard_map/all_gather | solution.py:17
  338.7 1.6 copy-start.5
  341.4 3.3 copy-start.1
  342.6 3.6 copy-start.2
  343.7 3.8 copy-start.3
  344.8 4.2 copy-start.4
  352.8 0.9 copy-start.7
  352.8 1.0 copy-start.11
  352.8 1.2 copy-start.12
  352.8 281.4 %all-reduce.3.cloned.1.call-start = ((), (), s32[]{:S(2)}) async-start(), calls=%async_computation.4 | async-start | bytes 229376
  363.5 9.7 %copy-start.6 = (f32[32,16,32]{2,1,0:T(8,128)}, f32[32,16,32]{2,1,0:T(8,128)S(1)}, u32[]{:S(2)}) copy-start(f32[32,16,32]{2,1,0:T(8,128)S(1)} %all-gather) | copy-start | bytes 196612
  519.8 22.8 %slice-start = ((f32[32,16,32]{2,1,0:T(8,128)}), f32[28,16,32]{2,1,0:T(8,128)S(1)}, s32[]{:S(2)}) async-start(f32[32,16,32]{2,1,0:T(8,128)} %copy-done.6), calls=%async_computation.5 | async-start | bytes 458752 | tf_op jit(solution)/shard_map/slice | solution.py:19
  594.6 5.3 copy-start.13
Sparse Core Ops, SparseCore 0:
  9.7 57.0 all-gather.7
  68.7 125.3 all-gather.9
  297.6 28.1 all-gather.11
  352.9 161.8 all-gather.13
  600.0 34.0 all-reduce.2
where the time goes:
time: 647 us; the launch traced here: 642 us
  waiting for transfers between devices  348 us (54%)
  matrix products  103 us (16%)
  local copies, waits for them, and re-layouts  84.8 us (13%)
  other arithmetic  49.3 us (8%)
  blocking collectives  39.3 us (6%)
  between operations  18.1 us (3%)
    all_gather x1, waiting for transfers between devices, joined(): pieces = jax.tree.map(lambda part: lax.all_gather(part, axis), value)  132 us
    all_gather x1, waiting for transfers between devices, on_device(): lax.all_gather(query_up, 'ctx', axis=0, tiled=True).astype(jnp.float32)  117 us
    all_gather x1, waiting for transfers between devices, on_device(): latent_full = lax.all_gather(latent_up, 'ctx', axis=0, tiled=True)  48.4 us
    add x7, other arithmetic, combine_states(): mixed_first * factor_first[..., None]  36.3 us
    unnamed x6, waiting for transfers between devices  33.8 us
    all_gather x1, local copies, waits for them, and re-layouts, on_device(): lax.all_gather(query_up, 'ctx', axis=0, tiled=True).astype(jnp.float32)  31 us
    dot_general x1, matrix products, on_device(): jnp.einsum('srq,qhe->srhe', query_input, query_map, preferred_element_typ...  26.8 us
    dot_general x1, matrix products, on_device(): jnp.einsum('nhd,khd->nhk', merged[:, :, :NOPE_DIM], key_weight, preferred...  24.9 us
  transfers between devices with their start and end apart: 5, of which 5 were waited for; matrix products, arithmetic and copies ran while one was open for 4% of the time, Pallas kernels for 0%

commit v1 on v0

--- a/solution.py
+++ b/solution.py
@@ -1,8 +1,11 @@
+import functools
 import math
 
 import jax
 import jax.numpy as jnp
 from jax import lax
+from jax.experimental import pallas as pl
+from jax.experimental.pallas import tpu as pltpu
 from jax.sharding import PartitionSpec as P
 
 LATENT = 512
@@ -55,7 +58,7 @@
     )
 
 
-def on_device(
+def on_device_general(
     query_input,
     new_latent,
     new_rotary,
@@ -181,6 +184,443 @@
     )
 
 
+MESH = pl.DeviceIdType.MESH
+BF16 = jnp.bfloat16
+F32 = jnp.float32
+VMEM_LIMIT = 56 * 2**20
+
+
+def vmem():
+    return pl.BlockSpec(memory_space=pltpu.VMEM)
+
+
+def anywhere():
+    return pl.BlockSpec(memory_space=pl.ANY)
+
+
+def matmul(left, right):
+    return jnp.dot(left, right, preferred_element_type=F32)
+
+
+def matmul_t(left, right):
+    return lax.dot_general(left, right, (((1,), (1,)), ((), ())), preferred_element_type=F32)
+
+
+def remote(src, dst, send, recv, axis, peer):
+    return pltpu.make_async_remote_copy(
+        src_ref=src,
+        dst_ref=dst,
+        send_sem=send,
+        recv_sem=recv,
+        device_id={axis: peer},
+        device_id_type=MESH,
+    )
+
+
+def greet(peers):
+    barrier = pltpu.get_barrier_semaphore()
+    for axis, peer in peers:
+        pl.semaphore_signal(barrier, inc=1, device_id={axis: peer}, device_id_type=MESH)
+    pl.semaphore_wait(barrier, len(peers))
+
+
+def block_of(device, chips):
+    return lax.rem(device, 2) * chips + device // 2
+
+
+def exchange_kernel(n, chips, wl, wq, pack, cache, rotary, wl_all, wq_all, pack_all, cache_o, rotary_o, send, recv, local):
+    me = lax.axis_index("ctx")
+    partner = lax.bitwise_xor(me, 1)
+    mine = block_of(me, chips)
+    own = [
+        pltpu.make_async_copy(wl.at[mine], wl_all.at[me], local.at[0]),
+        pltpu.make_async_copy(wq.at[mine], wq_all.at[me], local.at[1]),
+        pltpu.make_async_copy(pack, pack_all.at[me], local.at[2]),
+    ]
+    for copy in own:
+        copy.start()
+    peers = [lax.bitwise_xor(me, o) for o in range(1, n)]
+    greet([("ctx", peer) for peer in peers])
+    copies = []
+    order = [o for o in range(n - 1, 0, -1)]
+    for o in order:
+        peer = peers[o - 1]
+        theirs = block_of(peer, chips)
+        copies.append(remote(pack, pack_all.at[me], send.at[0, o], recv.at[0, o], "ctx", peer))
+        copies.append(remote(wl.at[theirs], wl_all.at[me], send.at[1, o], recv.at[1, o], "ctx", peer))
+        copies.append(remote(wq.at[theirs], wq_all.at[me], send.at[2, o], recv.at[2, o], "ctx", peer))
+    copies.append(remote(cache, cache_o, send.at[0, 0], recv.at[0, 0], "ctx", partner))
+    copies.append(remote(rotary, rotary_o, send.at[1, 0], recv.at[1, 0], "ctx", partner))
+    for copy in copies:
+        copy.start()
+    for copy in own:
+        copy.wait()
+    for copy in copies:
+        copy.wait()
+
+
+def query_kernel(n, half, wl, wq, qin, qin_a, qin_b, down_q, down_a, down_b, up_n, up_r, down_l, up_l, cosine, sine, q_out, v_out):
+    latent = wl.shape[0] * wl.shape[2]
+    weights = wl[:, 0].reshape(latent, wl.shape[3])
+    weights = (weights.astype(F32) + matmul(down_l[...], up_l[0])).astype(BF16)
+    nope = NOPE_DIM
+    v_out[0] = weights[:, nope:]
+    rank = n * 2 * half
+    plain = wq[:, 0, : 2 * half].reshape(rank, nope)
+    merged = (plain.astype(F32) + matmul(down_q[...], up_n[0])).astype(BF16)
+    absorbed = matmul_t(merged, weights[:, :nope]).astype(BF16)
+    q_out[0, :, : LATENT] = matmul(qin[...], absorbed).astype(BF16)
+    turned = wq[:, 0, 2 * half :].reshape(n * half, 2 * ROTARY)
+    first = (turned[:, :ROTARY].astype(F32) + matmul(down_a[...], up_r[0])).astype(BF16)
+    second = (turned[:, ROTARY:].astype(F32) + matmul(down_b[...], up_r[0])).astype(BF16)
+    raw = matmul(qin_a[...], first) + matmul(qin_b[...], second)
+    swapped = jnp.concatenate([raw[:, ROTARY // 2 :], raw[:, : ROTARY // 2]], axis=1)
+    turned_raw = raw * cosine[...] + swapped * sine[...]
+    q_out[0, :, LATENT:] = jnp.concatenate(
+        [turned_raw, jnp.zeros_like(turned_raw)], axis=1
+    ).astype(BF16)
+
+
+def attention_kernel(chips, hd, q, value, cache_a, rotary_a, cache_b, rotary_b, limit, new_key, mask, out, q_all, o_send, o_all, s_send, s_all, score_a, score_b, kept, qs, qr, os_, or_, ss, sr):
+    me = lax.axis_index("ctx")
+    core = lax.rem(me, 2)
+    scale = 1.0 / math.sqrt(NOPE_DIM + ROTARY)
+    peers = [lax.bitwise_xor(me, 2 * o) for o in range(1, chips)]
+    greet([("ctx", peer) for peer in peers])
+    outgoing = []
+    for o in range(chips - 1, 0, -1):
+        copy = remote(q, q_all.at[o - 1], qs.at[o - 1], qr.at[o - 1], "ctx", peers[o - 1])
+        copy.start()
+        outgoing.append(copy)
+    span = cache_a.shape[0]
+    rows = q.shape[0]
+
+    def attend(query, extra):
+        latent = query[:, :LATENT]
+        turned = query[:, LATENT : LATENT + ROTARY]
+        tops = []
+        for score, cache, rotary, device in (
+            (score_a, cache_a, rotary_a, me),
+            (score_b, cache_b, rotary_b, lax.bitwise_xor(me, 1)),
+        ):
+            part = (matmul_t(latent, cache[...]) + matmul(turned, rotary[...])) * scale
+            place = lax.broadcasted_iota(jnp.int32, (rows, span), 1) + device * span
+            part = jnp.where(place < limit[...], part, NEG)
+            score[...] = part
+            tops.append(jnp.max(part, axis=1, keepdims=True))
+        top = jnp.maximum(tops[0], tops[1])
+        if extra:
+            wide = matmul_t(query[...], new_key[...]) * scale
+            wide = jnp.where(mask[...] > 0, wide, NEG)
+            top = jnp.maximum(top, jnp.max(wide, axis=1, keepdims=True))
+        total = jnp.zeros((rows, 1), F32)
+        mixed = jnp.zeros((rows, LATENT), F32)
+        seen = top > 0.5 * NEG
+        for score, cache in ((score_a, cache_a), (score_b, cache_b)):
+            weight = jnp.where(seen, jnp.exp(score[...] - top), 0.0)
+            total = total + jnp.sum(weight, axis=1, keepdims=True)
+            mixed = mixed + matmul(weight.astype(BF16), cache[...])
+        if extra:
+            weight = jnp.exp(wide - top)
+            total = total + jnp.sum(weight, axis=1, keepdims=True)
+            mixed = mixed + matmul(weight.astype(BF16), new_key[:, :LATENT])
+        return top, total, mixed
+
+    top, total, mixed = attend(q, True)
+    kept[...] = mixed
+    lane = lax.broadcasted_iota(jnp.int32, (rows, 128), 1)
+    mine = jnp.where(lane == 0, top, total)
+    s_send[chips - 1] = mine
+
+    returns = []
+    for o in range(1, chips):
+        outgoing[chips - 1 - o].wait_recv()
+        top_o, total_o, mixed_o = attend(q_all.at[o - 1], False)
+        o_send[o - 1] = mixed_o.astype(BF16)
+        s_send[o - 1] = jnp.where(lane == 0, top_o, total_o)
+        for src, dst, send, recv in ((o_send, o_all, os_, or_), (s_send, s_all, ss, sr)):
+            copy = remote(src.at[o - 1], dst.at[o - 1], send.at[o - 1], recv.at[o - 1], "ctx", peers[o - 1])
+            copy.start()
+            returns.append(copy)
+    for copy in outgoing:
+        copy.wait_send()
+    for copy in returns:
+        copy.wait()
+    parts = [s_send[chips - 1]] + [s_all[o] for o in range(chips - 1)]
+    best = functools.reduce(jnp.maximum, [part[:, :1] for part in parts])
+    total = jnp.zeros((rows, 1), F32)
+    mixed = jnp.zeros((rows, LATENT), F32)
+    for index, part in enumerate(parts):
+        factor = jnp.exp(part[:, :1] - best)
+        total = total + part[:, 1:2] * factor
+        block = kept[...] if index == 0 else o_all[index - 1].astype(F32)
+        mixed = mixed + block * factor
+    kept[...] = mixed / total
+    each = rows // hd
+    for h in range(hd):
+        out[:, h * value.shape[2] : (h + 1) * value.shape[2]] = jnp.dot(
+            kept[h * each : (h + 1) * each, :],
+            value[h].astype(F32),
+            precision=lax.Precision.HIGHEST,
+            preferred_element_type=F32,
+        ).astype(BF16)
+
+
+def output_kernel(n, chips, nz, piece, weight, out, pieces, wide, partial, landed, ps, pr, zs, zr, ws):
+    me = lax.axis_index("ctx")
+    z = lax.axis_index("head")
+    depth = piece.shape[1]
+    loads = []
+    for g in range(n):
+        part = pl.ds(g * depth, depth)
+        copy = pltpu.make_async_copy(weight.at[part], wide.at[part], ws.at[g])
+        copy.start()
+        loads.append(copy)
+    peers = [lax.bitwise_xor(me, o) for o in range(1, n)]
+    planes = [lax.rem(z + o, nz) for o in range(1, nz)]
+    greet([("ctx", peer) for peer in peers] + [("head", plane) for plane in planes])
+    mine = block_of(me, chips)
+    copies = []
+    for o in range(n - 1, 0, -1):
+        copy = remote(piece, pieces.at[mine], ps.at[o - 1], pr.at[o - 1], "ctx", peers[o - 1])
+        copy.start()
+        copies.append(copy)
+    pieces[mine] = piece[...]
+    for copy in loads:
+        copy.wait()
+    for copy in copies:
+        copy.wait()
+    total = matmul(pieces[0], wide[:depth])
+    for g in range(1, n):
+        total = total + matmul(pieces[g], wide[g * depth : (g + 1) * depth])
+    rows = total.shape[0] // nz
+    for b in range(nz):
+        partial[b] = total[b * rows : (b + 1) * rows]
+    copies = []
+    for o in range(1, nz):
+        plane = planes[o - 1]
+        copy = remote(partial.at[plane], landed.at[o - 1], zs.at[o - 1], zr.at[o - 1], "head", plane)
+        copy.start()
+        copies.append(copy)
+    for copy in copies:
+        copy.wait()
+    result = partial[z]
+    for o in range(nz - 1):
+        result = result + landed[o]
+    out[...] = result.astype(BF16)
+
+
+def on_device_split(
+    n,
+    nz,
+    query_input,
+    new_latent,
+    new_rotary,
+    lengths,
+    adapter_index,
+    query_up,
+    latent_up,
+    query_adapter_down,
+    query_adapter_up,
+    latent_adapter_down,
+    latent_adapter_up,
+    cache_latent,
+    cache_rotary,
+    output_weight,
+):
+    chips = n // 2
+    steps, local_rows, rank = query_input.shape
+    rows = local_rows * n
+    band = rows // nz
+    heads = query_up.shape[1]
+    hd = heads // n
+    slab = query_up.shape[0]
+    half = slab // 2
+    latent_slab = latent_up.shape[0]
+    value_dim = latent_up.shape[2] - NOPE_DIM
+    model = output_weight.shape[1]
+    count = steps * rows
+    me = lax.axis_index("ctx")
+    first_head = block_of(me, chips) * hd
+
+    plain = jnp.transpose(query_up[:, :, :NOPE_DIM], (1, 0, 2))
+    turned = jnp.transpose(query_up[:, :, NOPE_DIM:], (1, 0, 2))
+    turned = jnp.concatenate([turned[:, :half], turned[:, half:]], axis=2)
+    wq = jnp.concatenate([plain, turned], axis=1).reshape(n, hd, 3 * half, NOPE_DIM)
+    wl = jnp.transpose(latent_up, (1, 0, 2)).reshape(n, hd, latent_slab, latent_up.shape[2])
+    width = rank + LATENT + ROTARY
+    padded = -(-width // 256) * 256
+    small = jnp.concatenate([query_input, new_latent, new_rotary], axis=2)
+    small = jnp.pad(small, ((0, 0), (0, 0), (0, padded - width)))
+    pack = small.reshape(16, steps * local_rows * padded // 16)
+
+    like = lambda value: jax.ShapeDtypeStruct(value.shape, value.dtype)
+    wl_all, wq_all, pack_all, cache_o, rotary_o = pl.pallas_call(
+        functools.partial(exchange_kernel, n, chips),
+        out_shape=[
+            like(wl),
+            like(wq),
+            jax.ShapeDtypeStruct((n,) + pack.shape, BF16),
+            like(cache_latent),
+            like(cache_rotary),
+        ],
+        in_specs=[anywhere()] * 5,
+        out_specs=[anywhere()] * 5,
+        scratch_shapes=[
+            pltpu.SemaphoreType.DMA((3, n)),
+            pltpu.SemaphoreType.DMA((3, n)),
+            pltpu.SemaphoreType.DMA((3,)),
+        ],
+        compiler_params=pltpu.CompilerParams(collective_id=0, has_side_effects=True),
+        name="exchange",
+    )(wl, wq, pack, cache_latent, cache_rotary)
+
+    def arranged(value):
+        value = value.reshape((steps, nz, band) + value.shape[2:])
+        value = jnp.moveaxis(value, 1, 0)
+        return value.reshape((count,) + value.shape[3:])
+
+    whole = pack_all.reshape(n, steps, local_rows, padded)
+    whole = jnp.moveaxis(whole, 0, 1).reshape(steps, rows, padded)
+    whole = arranged(whole)
+    qin = whole[:, :rank]
+    new_key = jnp.pad(whole[:, rank:width], ((0, 0), (0, ROTARY)))
+    split = qin.reshape(count, n, 2, half)
+    qin_a = split[:, :, 0].reshape(count, n * half)
+    qin_b = split[:, :, 1].reshape(count, n * half)
+
+    step_of = jnp.broadcast_to(jnp.arange(steps, dtype=jnp.int32)[:, None], (steps, rows))
+    row_of = jnp.broadcast_to(jnp.arange(rows, dtype=jnp.int32)[None, :], (steps, rows))
+    step_of = arranged(step_of)
+    row_of = arranged(row_of)
+    length_of = arranged(jnp.broadcast_to(lengths[None, :], (steps, rows)))
+    position = (length_of + step_of).astype(F32)[:, None]
+    freq = jnp.exp(
+        jnp.arange(ROTARY // 2, dtype=F32) * (-math.log(10000.0) / (ROTARY // 2))
+    )
+    angle = position * freq
+    cosine = jnp.concatenate([jnp.cos(angle)] * 2, axis=1)
+    sine = jnp.concatenate([-jnp.sin(angle), jnp.sin(angle)], axis=1)
+    mask = (row_of[:, None] == row_of[None, :]) & (step_of[None, :] <= step_of[:, None])
+    mask = jnp.tile(mask.astype(jnp.int32), (hd, 1))
+    limit = jnp.tile(length_of[:, None], (hd, 1))
+
+    chosen_query = adapter_index[0]
+    chosen_latent = adapter_index[1]
+    pick = lambda value, index: lax.dynamic_index_in_dim(value, index, 0, keepdims=False)
+    down_q = pick(query_adapter_down, chosen_query)
+    down_l = pick(latent_adapter_down, chosen_latent)
+    width_r = down_q.shape[1]
+
+    def own_heads(value, index):
+        taken = lax.dynamic_slice(
+            value, (index, 0, first_head, 0), (1, width_r, hd, value.shape[3])
+        )[0]
+        return jnp.transpose(taken, (1, 0, 2))
+
+    up_q = own_heads(query_adapter_up, chosen_query)
+    up_l = own_heads(latent_adapter_up, chosen_latent)
+    down_split = down_q.reshape(n, 2, half, width_r)
+    down_a = down_split[:, 0].reshape(n * half, width_r)
+    down_b = down_split[:, 1].reshape(n * half, width_r)
+
+    per_head = lambda value: pl.BlockSpec(
+        (1,) + value.shape[1:], lambda h: (h,) + (0,) * (value.ndim - 1)
+    )
+    same = lambda value: pl.BlockSpec(value.shape, lambda h: (0,) * value.ndim)
+    up_n, up_r = up_q[:, :, :NOPE_DIM], up_q[:, :, NOPE_DIM:]
+    key_width = LATENT + 2 * ROTARY
+    q, value = pl.pallas_call(
+        functools.partial(query_kernel, n, half),
+        grid=(hd,),
+        in_specs=[
+            pl.BlockSpec((n, 1) + wl.shape[2:], lambda h: (0, h, 0, 0)),
+            pl.BlockSpec((n, 1) + wq.shape[2:], lambda h: (0, h, 0, 0)),
+            same(qin),
+            same(qin_a),
+            same(qin_b),
+            same(down_q),
+            same(down_a),
+            same(down_b),
+            per_head(up_n),
+            per_head(up_r),
+            same(down_l),
+            per_head(up_l),
+            same(cosine),
+            same(sine),
+        ],
+        out_specs=[
+            pl.BlockSpec((1, count, key_width), lambda h: (h, 0, 0)),
+            pl.BlockSpec((1, n * latent_slab, value_dim), lambda h: (h, 0, 0)),
+        ],
+        out_shape=[
+            jax.ShapeDtypeStruct((hd, count, key_width), BF16),
+            jax.ShapeDtypeStruct((hd, n * latent_slab, value_dim), BF16),
+        ],
+        compiler_params=pltpu.CompilerParams(vmem_limit_bytes=VMEM_LIMIT),
+        name="queries",
+    )(wl_all, wq_all, qin, qin_a, qin_b, down_q, down_a, down_b, up_n, up_r, down_l, up_l, cosine, sine)
+    q = q.reshape(hd * count, key_width)
+
+    lines = hd * count
+    others = chips - 1
+    span = cache_latent.shape[0]
+    dma = lambda number: pltpu.SemaphoreType.DMA((number,))
+    piece = pl.pallas_call(
+        functools.partial(attention_kernel, chips, hd),
+        out_shape=jax.ShapeDtypeStruct((count, hd * value_dim), BF16),
+        in_specs=[vmem()] * 9,
+        out_specs=vmem(),
+        scratch_shapes=[
+            pltpu.VMEM((others, lines, key_width), BF16),
+            pltpu.VMEM((others, lines, LATENT), BF16),
+            pltpu.VMEM((others, lines, LATENT), BF16),
+            pltpu.VMEM((chips, lines, 128), F32),
+            pltpu.VMEM((others, lines, 128), F32),
+            pltpu.VMEM((lines, span), F32),
+            pltpu.VMEM((lines, span), F32),
+            pltpu.VMEM((lines, LATENT), F32),
+        ]
+        + [dma(others)] * 6,
+        compiler_params=pltpu.CompilerParams(
+            collective_id=1, has_side_effects=True, vmem_limit_bytes=VMEM_LIMIT
+        ),
+        name="attention",
+    )(q, value, cache_latent, cache_rotary, cache_o, rotary_o, limit, new_key, mask)
+
+    result = pl.pallas_call(
+        functools.partial(output_kernel, n, chips, nz),
+        out_shape=jax.ShapeDtypeStruct((count // nz, model), BF16),
+        in_specs=[vmem(), anywhere()],
+        out_specs=vmem(),
+        scratch_shapes=[
+            pltpu.VMEM((n, count, hd * value_dim), BF16),
+            pltpu.VMEM(output_weight.shape, BF16),
+            pltpu.VMEM((nz, count // nz, model), F32),
+            pltpu.VMEM((nz - 1, count // nz, model), F32),
+            dma(n - 1),
+            dma(n - 1),
+            dma(nz - 1),
+            dma(nz - 1),
+            dma(n),
+        ],
+        compiler_params=pltpu.CompilerParams(
+            collective_id=2, has_side_effects=True, vmem_limit_bytes=VMEM_LIMIT
+        ),
+        name="output",
+    )(piece, output_weight)
+    return result.reshape(steps, band, model)
+
+
+def on_device(n, nz, *arrays):
+    rows = arrays[0].shape[1] * n
+    heads = arrays[5].shape[1]
+    power = n >= 4 and n & (n - 1) == 0
+    if power and nz > 1 and heads % n == 0 and rows % nz == 0 and rows * arrays[0].shape[0] // nz % 16 == 0:
+        return on_device_split(n, nz, *arrays)
+    return on_device_general(*arrays)
+
+
 def solution(mesh):
     placed = (
         P(None, "ctx", None),
@@ -199,5 +639,6 @@
         P("head", "ctx"),
     )
     return jax.shard_map(
-        on_device, mesh=mesh, in_specs=placed, out_specs=P(None, "head", "ctx"), check_vma=False
-    )
+        functools.partial(on_device, mesh.shape["ctx"], mesh.shape["head"]),
+        mesh=mesh, in_specs=placed, out_specs=P(None, "head", "ctx"), check_vma=False
+    )

time: 647 us -> 157 us (0.24)
  waiting for transfers between devices: 348 us -> 0 us
  Pallas kernels: 0 us -> 123 us
  matrix products: 103 us -> 0 us
  local copies, waits for them, and re-layouts: 84.8 us -> 28 us
  other arithmetic: 49.3 us -> 1.73 us
  blocking collectives: 39.3 us -> 0 us
  between operations: 18.1 us -> 4.11 us
    all_gather x4 -> x0, waiting for transfers between devices: 314 us -> none  [the longest x1 132 us: joined(): pieces = jax.tree.map(lambda part: lax.all_gather(part, axis), value)]
    pallas_call x0 -> x4, Pallas kernels: none -> 123 us  [the longest x1 48 us: on_device_split(): pl.pallas_call(functools.partial(attention_kernel, chips, hd), out_shape=...]
    dot_general x21 -> x0, matrix products: 103 us -> none  [the longest x1 26.8 us: on_device(): jnp.einsum('srq,qhe->srhe', query_input, query_map, preferred_element_typ...]
    all_gather x4 -> x0, blocking collectives: 39.3 us -> none  [the longest x2 19.1 us: joined(): pieces = jax.tree.map(lambda part: lax.all_gather(part, axis), value)]
    slice x12 -> x10, local copies, waits for them, and re-layouts: 44.2 us -> 5.73 us  [the longest x1 1.49 us: on_device_split(): qin_b = split[:, :, 1].reshape(count, n * half)]
    add x16 -> x0, other arithmetic: 36.5 us -> none  [the longest x7 36.3 us: combine_states(): mixed_first * factor_first[..., None]]
    unnamed x6 -> x0, waiting for transfers between devices: 33.8 us -> none
    all_gather x1 -> x0, local copies, waits for them, and re-layouts: 31 us -> none  [on_device(): lax.all_gather(query_up, 'ctx', axis=0, tiled=True).astype(jnp.float32)]
  transfers between devices with their start and end apart: 5 -> 0, of which waited for: 5 -> 0; matrix products, arithmetic and copies ran while one was open for 4% -> 0% of each run, Pallas kernels for 0% -> 0%
where the time goes in v1:
time: 157 us; the launch traced here: 156 us
  Pallas kernels  123 us (78%)
  local copies, waits for them, and re-layouts  28 us (18%)
  between operations  4.11 us (3%)
  other arithmetic  1.73 us (1%)
    pallas_call x1, Pallas kernels, on_device_split(): pl.pallas_call(functools.partial(attention_kernel, chips, hd), out_shape=...  48 us
    pallas_call x1, Pallas kernels, on_device_split(): pl.pallas_call(functools.partial(exchange_kernel, n, chips), out_shape=[l...  46 us
    pallas_call x1, Pallas kernels, on_device_split(): pl.pallas_call(functools.partial(output_kernel, n, chips, nz), out_shape=...  20 us
    pallas_call x1, Pallas kernels, on_device_split(): pl.pallas_call(functools.partial(query_kernel, n, half), grid=(hd,), in_s...  8.62 us

profile of v1, /device:TPU:0, one launch (start us, length us, event | category | flops | bytes accessed | tf_op | source)
XLA Modules:
  0.0 156.4 jit_solution(2558239448768084123)
XLA Ops:
  0.0 0.0 copy-start
  0.0 3.0 %copy.21 = bf16[32,64,256]{2,1,0:T(8,128)(2,1)} copy(bf16[32,64,256]{2,0,1:T(8,128)(2,1)} %bitcast.36) | data formatting | bytes 2097152 | tf_op jit(solution)/shard_map/transpose | solution.py:450
  3.0 1.7 %slice_bitcast_fusion = bf16[32,192,64]{2,0,1:T(8,128)(2,1)S(1)} fusion(bf16[192,32,192]{2,1,0:T(8,128)(2,1)} %param.19), kind=kLoop, calls=%fused_computation.1 | loop fusion | bytes 1572864 | tf_op jit(solution)/shard_map/transpose | solution.py:447
  4.7 0.0 copy-start.1
  4.7 0.3 fusion.6
  5.0 1.6 %copy-done.1 = bf16[192,32,192]{2,1,0:T(8,128)(2,1)S(1)} copy-done((bf16[192,32,192]{2,1,0:T(8,128)(2,1)S(1)}, bf16[192,32,192]{2,1,0:T(8,128)(2,1)}, u32[]{:S(2)}) %copy-start.1) | copy-done | bytes 2359320
  6.6 0.4 slice_bitcast_fusion.1
  6.9 0.7 maximum_maximum_fusion
  7.6 0.0 copy-start.3
  7.6 0.0 copy-start.4
  7.6 0.0 copy-start.5
  7.7 2.3 %copy.22 = bf16[32,288,128]{2,1,0:T(8,128)(2,1)} copy(bf16[32,288,128]{2,0,1:T(8,128)(2,1)S(1)} %maximum_maximum_fusion) | data formatting | bytes 4718592 | tf_op jit(solution)/shard_map/concatenate | solution.py:449
  10.0 0.0 copy-done.3
  10.0 0.0 copy-done.4
  10.0 0.0 copy-done.5
  10.0 0.6 reshape.146.pack
  10.7 46.0 %exchange.1 = (bf16[8,4,64,256]{3,2,1,0:T(8,128)(2,1)}, bf16[8,4,288,128]{3,2,1,0:T(8,128)(2,1)}, bf16[8,16,1152]{2,1,0:T(8,128)(2,1)}, bf16[2048,512]{1,0:T(8,128)(2,1)}, bf16[64,2048]{1,0:T(8,128)(2,1)}) custom-call(bf16[8,4,64,256]{3,2,1,0:T(8,128)(2,1)} %bitcast.33, bf16[8,4,288,128]{3,2,1,0:T(8,128)(2,1)} %bitcast.32, bf16[16,1152]{1,0:T(8,128)(2,1)} %reshape.146.pack, ...), custom_call_target="tpu_custom_call" | custom-call | tf_op jit(solution)/shard_map/exchange/pallas_call | solution.py:458
  56.6 0.0 copy-start.6
  56.7 1.2 reshape.147
  57.8 0.1 copy.23
  57.9 0.1 copy.24
  58.1 0.1 reshape.148
  58.2 0.0 copy-start.2
  58.2 0.2 reshape.149
  58.4 1.5 slice_reduce_fusion
  59.9 0.8 reshape_squeeze.12.qin_a
  60.7 0.8 reshape_squeeze.13.qin_b
  61.5 0.0 copy-done.6
  61.5 0.6 fusion.8
  64.0 0.0 copy-done
  64.0 0.0 copy-start.7
  64.0 0.9 copy.27
  65.0 0.2 reshape.150
  65.2 0.4 fusion.7
  65.6 0.9 copy.28
  66.4 0.8 copy.29
  67.3 0.0 copy-done.2
  67.3 1.0 constant_dynamic-slice_fusion.2
  68.3 0.6 slice.63.up_n
  69.0 0.6 slice.64.up_r
  71.6 0.8 constant_dynamic-slice_fusion.1
  72.4 0.7 copy.31
  73.2 1.0 constant_dynamic-slice_fusion
  74.2 0.7 copy.38
  74.9 0.0 copy-done.7
  74.9 0.1 broadcast_in_dim.8
  75.0 0.1 reshape.151
  75.1 0.1 reshape.152
  75.2 0.2 fusion.5
  75.4 0.7 pad_maximum_fusion
  76.1 8.6 %queries.1 = (bf16[4,64,640]{2,1,0:T(8,128)(2,1)}, bf16[4,512,128]{2,1,0:T(8,128)(2,1)}) custom-call(bf16[8,4,64,256]{3,2,1,0:T(8,128)(2,1)} %get-tuple-element.12.wl, bf16[8,4,288,128]{3,2,1,0:T(8,128)(2,1)} %get-tuple-element.13.wq, bf16[64,1536]{1,0:T(8,128)(2,1)} %copy-done.2, bf16[64,768]{1,0:T(8,128)(2,1)} %reshape_squeeze.12.qin_a, ...), custom_call_target="tpu_custom_call" | custom-call | tf_op jit(solution)/shard_map/queries/pallas_call | solution.py:533
  84.7 0.8 tile.21.limit
  85.5 0.6 pad.9.new_key
  86.2 0.1 eq.19
  86.3 0.1 and_convert_fusion
  86.4 0.7 tile.19
  87.0 48.0 %attention.1.piece = bf16[64,512]{1,0:T(8,128)(2,1)} custom-call(bf16[256,640]{1,0:T(8,128)(2,1)} %bitcast.44, bf16[4,512,128]{2,1,0:T(8,128)(2,1)} %get-tuple-element.16.value, bf16[2048,512]{1,0:T(8,128)(2,1)} %cache_a.1, bf16[64,2048]{1,0:T(8,128)(2,1)} %rotary_a.1, bf16[2048,512]{1,0:T(8,128)(2,1)} %get-tuple-element.17.cache_b, ...), custom_call_target="tpu_custom_call" | custom-call | tf_op jit(solution)/shard_map/attention/pallas_call | solution.py:569
  135.0 20.0 %output.1 = bf16[16,896]{1,0:T(8,128)(2,1)} custom-call(bf16[64,512]{1,0:T(8,128)(2,1)} %attention.1.piece, bf16[4096,896]{1,0:T(8,128)(2,1)} %weight.1), custom_call_target="tpu_custom_call" | custom-call | tf_op jit(solution)/shard_map/output/pallas_call | solution.py:591
  155.1 1.4 reshape.154
  (12 shorter events, 0.1 us)
Async XLA Ops:
  0.0 64.0 %copy-start = (bf16[8,1536,64]{1,2,0:T(8,128)(2,1)S(1)}, bf16[8,1536,64]{1,2,0:T(8,128)(2,1)}, u32[]{:S(2)}) copy-start(bf16[8,1536,64]{1,2,0:T(8,128)(2,1)} %param.21) | copy-start | bytes 4718596
  4.7 1.9 %copy-start.1 = (bf16[192,32,192]{2,1,0:T(8,128)(2,1)S(1)}, bf16[192,32,192]{2,1,0:T(8,128)(2,1)}, u32[]{:S(2)}) copy-start(bf16[192,32,192]{2,1,0:T(8,128)(2,1)} %param.19) | copy-start | bytes 7077892
  7.6 2.4 %copy-start.3 = (bf16[4,2,1536]{2,1,0:T(2,128)(2,1)S(1)}, bf16[4,2,1536]{2,1,0:T(2,128)(2,1)}, u32[]{:S(2)}) copy-start(bf16[4,2,1536]{2,1,0:T(2,128)(2,1)} %param.14) | copy-start | bytes 73732
  7.6 2.4 %copy-start.4 = (bf16[4,2,512]{2,1,0:T(2,128)(2,1)S(1)}, bf16[4,2,512]{2,1,0:T(2,128)(2,1)}, u32[]{:S(2)}) copy-start(bf16[4,2,512]{2,1,0:T(2,128)(2,1)} %param.15) | copy-start | bytes 24580
  7.6 2.3 %copy-start.5 = (bf16[4,2,64]{2,1,0:T(2,128)(2,1)S(1)}, bf16[4,2,64]{2,1,0:T(2,128)(2,1)}, u32[]{:S(2)}) copy-start(bf16[4,2,64]{2,1,0:T(2,128)(2,1)} %param.16) | copy-start | bytes 3076
  56.6 4.8 %copy-start.6 = (s32[2]{0:T(128)S(1)}, s32[2]{0:T(128)}, u32[]{:S(2)}) copy-start(s32[2]{0:T(128)} %param.18) | copy-start | bytes 28
  58.2 9.1 %copy-start.2 = (bf16[64,1536]{1,0:T(8,128)(2,1)}, bf16[64,1536]{1,0:T(8,128)(2,1)S(1)}, u32[]{:S(2)}) copy-start(bf16[64,1536]{1,0:T(8,128)(2,1)S(1)} %slice.58.qin) | copy-start | bytes 589828
  64.0 10.9 %copy-start.7 = (s32[16]{0:T(128)S(1)}, s32[16]{0:T(128)}, u32[]{:S(2)}) copy-start(s32[16]{0:T(128)} %param.17) | copy-start | bytes 196

commit v2 on v0

--- a/solution.py
+++ b/solution.py
@@ -1,8 +1,11 @@
+import functools
 import math
 
 import jax
 import jax.numpy as jnp
 from jax import lax
+from jax.experimental import pallas as pl
+from jax.experimental.pallas import tpu as pltpu
 from jax.sharding import PartitionSpec as P
 
 LATENT = 512
@@ -55,7 +58,7 @@
     )
 
 
-def on_device(
+def on_device_general(
     query_input,
     new_latent,
     new_rotary,
@@ -181,6 +184,432 @@
     )
 
 
+MESH = pl.DeviceIdType.MESH
+BF16 = jnp.bfloat16
+F32 = jnp.float32
+VMEM_LIMIT = 56 * 2**20
+
+
+def vmem():
+    return pl.BlockSpec(memory_space=pltpu.VMEM)
+
+
+def anywhere():
+    return pl.BlockSpec(memory_space=pl.ANY)
+
+
+def matmul(left, right):
+    return jnp.dot(left, right, preferred_element_type=F32)
+
+
+def matmul_t(left, right):
+    return lax.dot_general(left, right, (((1,), (1,)), ((), ())), preferred_element_type=F32)
+
+
+def remote(src, dst, send, recv, axis, peer):
+    return pltpu.make_async_remote_copy(
+        src_ref=src,
+        dst_ref=dst,
+        send_sem=send,
+        recv_sem=recv,
+        device_id={axis: peer},
+        device_id_type=MESH,
+    )
+
+
+def greet(peers):
+    barrier = pltpu.get_barrier_semaphore()
+    for axis, peer in peers:
+        pl.semaphore_signal(barrier, inc=1, device_id={axis: peer}, device_id_type=MESH)
+    pl.semaphore_wait(barrier, len(peers))
+
+
+def block_of(device, chips):
+    return lax.rem(device, 2) * chips + device // 2
+
+
+def fused_kernel(
+    n, chips, nz, hd,
+    key, plain, turned, pack, val, cache, rotary, weight, down_q, up_q, down_l, up_l, cosine, sine, limit, mask,
+    out,
+    key_all, plain_all, turned_all, pack_all, val_all, cache_o, rotary_o, wide, q, q_all, o_send, o_all, s_send, s_all,
+    s_own, score_a, score_b, kept, piece, pieces, partial, landed, qin, new_key,
+    ks, kr, ws, wr, ts, tr, ps, pr, vs, vr, cs, cr, qs, qr, os_, or_, ss, sr, hs, hr, zs, zr, local, loads_sem,
+):
+    me = lax.axis_index("ctx")
+    z = lax.axis_index("head")
+    partner = lax.bitwise_xor(me, 1)
+    mine = block_of(me, chips)
+    groups = hd // 2
+    scale = 1.0 / math.sqrt(NOPE_DIM + ROTARY)
+    span = cache_o.shape[0]
+    count = cosine.shape[0]
+    rows = 2 * count
+    rank = down_q.shape[0]
+    latent = down_l.shape[0]
+
+    own = [
+        pltpu.make_async_copy(key.at[mine], key_all.at[me], local.at[0]),
+        pltpu.make_async_copy(plain.at[mine], plain_all.at[me], local.at[1]),
+        pltpu.make_async_copy(turned.at[mine], turned_all.at[me], local.at[2]),
+        pltpu.make_async_copy(pack, pack_all.at[me], local.at[3]),
+        pltpu.make_async_copy(val.at[mine], val_all.at[me], local.at[4]),
+    ]
+    for copy in own:
+        copy.start()
+    peers = [lax.bitwise_xor(me, o) for o in range(1, n)]
+    planes = [lax.rem(z + o, nz) for o in range(1, nz)]
+    greet([("ctx", peer) for peer in peers] + [("head", plane) for plane in planes])
+
+    order = range(n - 1, 0, -1)
+    swaps = [
+        remote(cache, cache_o, cs.at[0], cr.at[0], "ctx", partner),
+        remote(rotary, rotary_o, cs.at[1], cr.at[1], "ctx", partner),
+    ]
+    firsts = []
+    for o in order:
+        peer = peers[o - 1]
+        firsts.append(remote(pack, pack_all.at[me], ps.at[o], pr.at[o], "ctx", peer))
+        firsts.append(remote(key.at[block_of(peer, chips)], key_all.at[me], ks.at[o], kr.at[o], "ctx", peer))
+
+    def group_copies(g):
+        heads = pl.ds(g * 2, 2)
+        copies = []
+        for o in order:
+            peer = peers[o - 1]
+            theirs = block_of(peer, chips)
+            copies.append(
+                remote(plain.at[theirs, heads], plain_all.at[me, heads], ws.at[g, o], wr.at[g, o], "ctx", peer)
+            )
+            copies.append(
+                remote(turned.at[theirs, heads], turned_all.at[me, heads], ts.at[g, o], tr.at[g, o], "ctx", peer)
+            )
+        return copies
+
+    values = [
+        remote(val.at[block_of(peers[o - 1], chips)], val_all.at[me], vs.at[o], vr.at[o], "ctx", peers[o - 1])
+        for o in order
+    ]
+    for copy in firsts:
+        copy.start()
+    for g in range(groups):
+        for copy in group_copies(g):
+            copy.start()
+        if g == 0:
+            for copy in swaps:
+                copy.start()
+    for copy in values:
+        copy.start()
+    loads = []
+    depth = piece.shape[1]
+    for g in range(n):
+        part = pl.ds(g * depth, depth)
+        copy = pltpu.make_async_copy(weight.at[part], wide.at[part], loads_sem.at[g])
+        copy.start()
+        loads.append(copy)
+
+    for copy in own:
+        copy.wait()
+    for copy in firsts:
+        copy.wait()
+    small = pack_all[...].reshape(count, pack_all.shape[2]).astype(BF16)
+    qin[...] = small[:, :rank]
+    new_key[...] = jnp.concatenate(
+        [small[:, rank : rank + LATENT + ROTARY], jnp.zeros((count, ROTARY), BF16)], axis=1
+    )
+
+    def attend(query, extra):
+        queries = query[:, :LATENT]
+        rotated = query[:, LATENT : LATENT + ROTARY]
+        tops = []
+        for score, held, turn, device in (
+            (score_a, cache, rotary, me),
+            (score_b, cache_o, rotary_o, partner),
+        ):
+            part = (matmul_t(queries, held[...]) + matmul(rotated, turn[...])) * scale
+            place = lax.broadcasted_iota(jnp.int32, (rows, span), 1)
+            part = jnp.where(place < limit[...] - device * span, part, NEG)
+            score[...] = part
+            tops.append(jnp.max(part, axis=1, keepdims=True))
+        top = jnp.maximum(tops[0], tops[1])
+        if extra:
+            own_score = matmul_t(query, new_key[...]) * scale
+            own_score = jnp.where(mask[...] > 0, own_score, NEG)
+            top = jnp.maximum(top, jnp.max(own_score, axis=1, keepdims=True))
+        shift = jnp.where(top > 0.5 * NEG, top, 0.0)
+        total = jnp.zeros((rows, 1), F32)
+        mixed = jnp.zeros((rows, LATENT), F32)
+        for score, held in ((score_a, cache), (score_b, cache_o)):
+            share = jnp.exp(score[...] - shift)
+            total = total + jnp.sum(share, axis=1, keepdims=True)
+            mixed = mixed + matmul(share.astype(BF16), held[...])
+        if extra:
+            share = jnp.exp(own_score - shift)
+            total = total + jnp.sum(share, axis=1, keepdims=True)
+            mixed = mixed + matmul(share.astype(BF16), new_key[:, :LATENT])
+        return top, total, mixed
+
+    lane = lax.broadcasted_iota(jnp.int32, (rows, 128), 1)
+
+    def query_copy(o, g):
+        peer = lax.bitwise_xor(me, 2 * (o + 1))
+        return remote(q.at[g], q_all.at[o, g], qs.at[o, g], qr.at[o, g], "ctx", peer)
+
+    def own_group(g, carry):
+        for copy in group_copies(g):
+            copy.wait()
+        for i in range(2):
+            h = g * 2 + i
+            weights = key_all[:, h].reshape(latent, NOPE_DIM).astype(F32)
+            weights = (weights + matmul(down_l[...], up_l[h, :, :NOPE_DIM])).astype(BF16)
+            delta = matmul(down_q[...], up_q[h])
+            base = plain_all[:, h].reshape(rank, NOPE_DIM).astype(F32)
+            merged = (base + delta[:, :NOPE_DIM]).astype(BF16)
+            absorbed = matmul_t(merged, weights).astype(BF16)
+            lines = pl.ds(i * count, count)
+            q[g, lines, :LATENT] = matmul(qin[...], absorbed).astype(BF16)
+            halves = turned_all[:, h].astype(F32)
+            base = jnp.concatenate([halves[:, :, :ROTARY], halves[:, :, ROTARY:]], axis=1)
+            merged = (base.reshape(rank, ROTARY) + delta[:, NOPE_DIM:]).astype(BF16)
+            raw = matmul(qin[...], merged)
+            swapped = jnp.concatenate([raw[:, ROTARY // 2 :], raw[:, : ROTARY // 2]], axis=1)
+            spun = raw * cosine[...] + swapped * sine[...]
+            q[g, lines, LATENT:] = jnp.concatenate([spun, jnp.zeros_like(spun)], axis=1).astype(BF16)
+        for o in range(chips - 2, -1, -1):
+            query_copy(o, g).start()
+
+        @pl.when(g == 0)
+        def _():
+            for copy in swaps:
+                copy.wait()
+
+        top, total, mixed = attend(q[g], True)
+        kept[g] = mixed
+        s_own[g] = jnp.where(lane == 0, top, total)
+        return carry
+
+    lax.fori_loop(0, groups, own_group, 0)
+
+    def return_copies(o, g):
+        peer = lax.bitwise_xor(me, 2 * (o + 1))
+        return (
+            remote(o_send.at[o, g], o_all.at[o, g], os_.at[o, g], or_.at[o, g], "ctx", peer),
+            remote(s_send.at[o, g], s_all.at[o, g], ss.at[o, g], sr.at[o, g], "ctx", peer),
+        )
+
+    def peer_group(t, carry):
+        g = t // (chips - 1)
+        o = chips - 2 - t % (chips - 1)
+        query_copy(o, g).wait()
+        top, total, mixed = attend(q_all[o, g], False)
+        o_send[o, g] = mixed.astype(BF16)
+        s_send[o, g] = jnp.where(lane == 0, top, total)
+        for copy in return_copies(o, g):
+            copy.start()
+        return carry
+
+    lax.fori_loop(0, groups * (chips - 1), peer_group, 0)
+    for copy in values:
+        copy.wait()
+    for g in range(groups):
+        for o in range(chips - 2, -1, -1):
+            for copy in return_copies(o, g):
+                copy.wait()
+        parts = [s_own[g]] + [s_all[o, g] for o in range(chips - 1)]
+        best = functools.reduce(jnp.maximum, [part[:, :1] for part in parts])
+        total = jnp.zeros((rows, 1), F32)
+        mixed = jnp.zeros((rows, LATENT), F32)
+        for index, part in enumerate(parts):
+            factor = jnp.exp(part[:, :1] - best)
+            total = total + part[:, 1:2] * factor
+            block = kept[g] if index == 0 else o_all[index - 1, g].astype(F32)
+            mixed = mixed + block * factor
+        kept[g] = mixed / total
+        for i in range(2):
+            h = g * 2 + i
+            width = val_all.shape[3]
+            weights = val_all[:, h].reshape(latent, width).astype(F32)
+            weights = (weights + matmul(down_l[...], up_l[h, :, NOPE_DIM:])).astype(BF16)
+            piece[:, h * width : (h + 1) * width] = jnp.dot(
+                kept[g, i * count : (i + 1) * count, :],
+                weights.astype(F32),
+                precision=lax.Precision.HIGHEST,
+                preferred_element_type=F32,
+            ).astype(BF16)
+
+    copies = []
+    for o in order:
+        copy = remote(piece, pieces.at[mine], hs.at[o], hr.at[o], "ctx", peers[o - 1])
+        copy.start()
+        copies.append(copy)
+    pieces[mine] = piece[...]
+    for copy in loads:
+        copy.wait()
+    for copy in copies:
+        copy.wait()
+    total = matmul(pieces[0], wide[:depth])
+    for g in range(1, n):
+        total = total + matmul(pieces[g], wide[g * depth : (g + 1) * depth])
+    band = total.shape[0] // nz
+    for b in range(nz):
+        partial[b] = total[b * band : (b + 1) * band]
+    copies = []
+    for o in range(1, nz):
+        plane = planes[o - 1]
+        copy = remote(partial.at[plane], landed.at[o - 1], zs.at[o - 1], zr.at[o - 1], "head", plane)
+        copy.start()
+        copies.append(copy)
+    for copy in copies:
+        copy.wait()
+    result = partial[z]
+    for o in range(nz - 1):
+        result = result + landed[o]
+    out[...] = result.astype(BF16)
+
+
+def on_device_split(
+    n,
+    nz,
+    query_input,
+    new_latent,
+    new_rotary,
+    lengths,
+    adapter_index,
+    query_up,
+    latent_up,
+    query_adapter_down,
+    query_adapter_up,
+    latent_adapter_down,
+    latent_adapter_up,
+    cache_latent,
+    cache_rotary,
+    output_weight,
+):
+    chips = n // 2
+    steps, local_rows, rank = query_input.shape
+    band = local_rows * n // nz
+    heads = query_up.shape[1]
+    hd = heads // n
+    groups = hd // 2
+    slab = query_up.shape[0]
+    half = slab // 2
+    latent_slab = latent_up.shape[0]
+    value_dim = latent_up.shape[2] - NOPE_DIM
+    model = output_weight.shape[1]
+    count = steps * local_rows * n
+    me = lax.axis_index("ctx")
+    first_head = block_of(me, chips) * hd
+
+    plain = jnp.transpose(query_up[:, :, :NOPE_DIM], (1, 0, 2)).reshape(n, hd, slab, NOPE_DIM)
+    turned = jnp.transpose(query_up[:, :, NOPE_DIM:], (1, 0, 2))
+    turned = jnp.concatenate([turned[:, :half], turned[:, half:]], axis=2)
+    turned = turned.reshape(n, hd, half, 2 * ROTARY)
+    latents = jnp.transpose(latent_up, (1, 0, 2)).reshape(n, hd, latent_slab, latent_up.shape[2])
+    key, val = latents[..., :NOPE_DIM], latents[..., NOPE_DIM:]
+    small = jnp.concatenate([query_input, new_latent, new_rotary], axis=2).astype(F32)
+    small = small.reshape(steps * local_rows, small.shape[2])
+    pack = jnp.pad(small, ((0, 0), (0, -small.shape[1] % 128)))
+
+    spread = lambda value: jnp.broadcast_to(value, (n, steps, local_rows)).reshape(count)
+    step_of = spread(jnp.arange(steps, dtype=jnp.int32)[None, :, None])
+    row_of = spread(
+        jnp.arange(n * local_rows, dtype=jnp.int32).reshape(n, 1, local_rows)
+    )
+    length_of = spread(lengths.reshape(n, 1, local_rows))
+    position = (length_of + step_of).astype(F32)[:, None]
+    freq = jnp.exp(
+        jnp.arange(ROTARY // 2, dtype=F32) * (-math.log(10000.0) / (ROTARY // 2))
+    )
+    angle = position * freq
+    cosine = jnp.concatenate([jnp.cos(angle)] * 2, axis=1)
+    sine = jnp.concatenate([-jnp.sin(angle), jnp.sin(angle)], axis=1)
+    mask = (row_of[:, None] == row_of[None, :]) & (step_of[None, :] <= step_of[:, None])
+    mask = jnp.tile(mask.astype(jnp.int32), (2, 1))
+    limit = jnp.tile(length_of[:, None], (2, 1))
+
+    chosen_query = adapter_index[0]
+    chosen_latent = adapter_index[1]
+    pick = lambda value, index: lax.dynamic_index_in_dim(value, index, 0, keepdims=False)
+    down_q = pick(query_adapter_down, chosen_query)
+    down_l = pick(latent_adapter_down, chosen_latent)
+    width_r = down_q.shape[1]
+
+    def own_heads(value, index):
+        taken = lax.dynamic_slice(
+            value, (index, 0, first_head, 0), (1, width_r, hd, value.shape[3])
+        )[0]
+        return jnp.transpose(taken, (1, 0, 2))
+
+    up_q = own_heads(query_adapter_up, chosen_query)
+    up_l = own_heads(latent_adapter_up, chosen_latent)
+
+    key_width = LATENT + 2 * ROTARY
+    lines = 2 * count
+    others = chips - 1
+    span = cache_latent.shape[0]
+    dma = lambda *number: pltpu.SemaphoreType.DMA(number)
+    store = lambda kind, *shape: pltpu.VMEM(shape, kind)
+    result = pl.pallas_call(
+        functools.partial(fused_kernel, n, chips, nz, hd),
+        out_shape=jax.ShapeDtypeStruct((count // nz, model), BF16),
+        in_specs=[anywhere()] * 5 + [vmem()] * 2 + [anywhere()] + [vmem()] * 8,
+        out_specs=vmem(),
+        scratch_shapes=[
+            store(BF16, *key.shape),
+            store(BF16, *plain.shape),
+            store(BF16, *turned.shape),
+            store(F32, n, *pack.shape),
+            store(BF16, *val.shape),
+            store(BF16, *cache_latent.shape),
+            store(BF16, *cache_rotary.shape),
+            store(BF16, *output_weight.shape),
+            store(BF16, groups, lines, key_width),
+            store(BF16, others, groups, lines, key_width),
+            store(BF16, others, groups, lines, LATENT),
+            store(BF16, others, groups, lines, LATENT),
+            store(F32, others, groups, lines, 128),
+            store(F32, others, groups, lines, 128),
+            store(F32, groups, lines, 128),
+            store(F32, lines, span),
+            store(F32, lines, span),
+            store(F32, groups, lines, LATENT),
+            store(BF16, count, hd * value_dim),
+            store(BF16, n, count, hd * value_dim),
+            store(F32, nz, count // nz, model),
+            store(F32, nz - 1, count // nz, model),
+            store(BF16, count, rank),
+            store(BF16, count, key_width),
+        ]
+        + [dma(n)] * 2
+        + [dma(groups, n)] * 4
+        + [dma(n)] * 4
+        + [dma(2)] * 2
+        + [dma(others, groups)] * 6
+        + [dma(n)] * 2
+        + [dma(nz - 1)] * 2
+        + [dma(5), dma(n)],
+        compiler_params=pltpu.CompilerParams(
+            collective_id=0, has_side_effects=True, vmem_limit_bytes=VMEM_LIMIT
+        ),
+        name="fused",
+    )(
+        key, plain, turned, pack, val, cache_latent, cache_rotary, output_weight,
+        down_q, up_q, down_l, up_l, cosine, sine, limit, mask,
+    )
+    devices = band // local_rows
+    result = result.reshape(devices, steps, local_rows, model)
+    return jnp.transpose(result, (1, 0, 2, 3)).reshape(steps, band, model)
+
+
+def on_device(n, nz, *arrays):
+    rows = arrays[0].shape[1] * n
+    heads = arrays[5].shape[1]
+    power = n >= 4 and n & (n - 1) == 0
+    if power and nz > 1 and heads % (2 * n) == 0 and rows % nz == 0 and rows // nz % arrays[0].shape[1] == 0 and rows * arrays[0].shape[0] // nz % 16 == 0:
+        return on_device_split(n, nz, *arrays)
+    return on_device_general(*arrays)
+
+
 def solution(mesh):
     placed = (
         P(None, "ctx", None),
@@ -199,5 +628,6 @@
         P("head", "ctx"),
     )
     return jax.shard_map(
-        on_device, mesh=mesh, in_specs=placed, out_specs=P(None, "head", "ctx"), check_vma=False
-    )
+        functools.partial(on_device, mesh.shape["ctx"], mesh.shape["head"]),
+        mesh=mesh, in_specs=placed, out_specs=P(None, "head", "ctx"), check_vma=False
+    )

time: 647 us -> 124 us (0.19)
  waiting for transfers between devices: 348 us -> 0 us
  matrix products: 103 us -> 0 us
  Pallas kernels: 0 us -> 101 us
  local copies, waits for them, and re-layouts: 84.8 us -> 17 us
  other arithmetic: 49.3 us -> 2.08 us
  blocking collectives: 39.3 us -> 0 us
  between operations: 18.1 us -> 3.99 us
    all_gather x4 -> x0, waiting for transfers between devices: 314 us -> none  [the longest x1 132 us: joined(): pieces = jax.tree.map(lambda part: lax.all_gather(part, axis), value)]
    dot_general x21 -> x0, matrix products: 103 us -> none  [the longest x1 26.8 us: on_device(): jnp.einsum('srq,qhe->srhe', query_input, query_map, preferred_element_typ...]
    pallas_call x0 -> x1, Pallas kernels: none -> 101 us  [on_device_split(): pl.pallas_call(functools.partial(fused_kernel, n, chips, nz, hd), out_sha...]
    slice x12 -> x3, local copies, waits for them, and re-layouts: 44.2 us -> 2.15 us  [the longest x1 1.3 us: on_device_split(): key, val = (latents[..., :NOPE_DIM], latents[..., NOPE_DIM:])]
    all_gather x4 -> x0, blocking collectives: 39.3 us -> none  [the longest x2 19.1 us: joined(): pieces = jax.tree.map(lambda part: lax.all_gather(part, axis), value)]
    add x16 -> x0, other arithmetic: 36.5 us -> none  [the longest x7 36.3 us: combine_states(): mixed_first * factor_first[..., None]]
    unnamed x6 -> x0, waiting for transfers between devices: 33.8 us -> none
    all_gather x1 -> x0, local copies, waits for them, and re-layouts: 31 us -> none  [on_device(): lax.all_gather(query_up, 'ctx', axis=0, tiled=True).astype(jnp.float32)]
  transfers between devices with their start and end apart: 5 -> 0, of which waited for: 5 -> 0; matrix products, arithmetic and copies ran while one was open for 4% -> 0% of each run, Pallas kernels for 0% -> 0%
where the time goes in v2:
time: 124 us
  Pallas kernels  101 us (81%)
  local copies, waits for them, and re-layouts  17 us (14%)
  between operations  3.99 us (3%)
  other arithmetic  2.08 us (2%)
    pallas_call x1, Pallas kernels, on_device_split(): pl.pallas_call(functools.partial(fused_kernel, n, chips, nz, hd), out_sha...  101 us
    dynamic_slice x4, local copies, waits for them, and re-layouts, own_heads(): lax.dynamic_slice(value, (index, 0, first_head, 0), (1, width_r, hd, valu...  3.37 us
    dynamic_slice x4, local copies, waits for them, and re-layouts, on_device_split(): lax.dynamic_index_in_dim(value, index, 0, keepdims=False)  2.55 us

profile of v2, /device:TPU:0, one launch (start us, length us, event | category | flops | bytes accessed | tf_op | source)
XLA Modules:
  0.0 124.0 jit_solution(12202717579047599398)
XLA Ops:
  0.0 0.0 copy-start
  0.0 0.0 copy-start.1
  0.0 2.0 %copy.24 = bf16[32,64,256]{2,1,0:T(8,128)(2,1)S(1)} copy(bf16[32,64,256]{2,0,1:T(8,128)(2,1)} %bitcast.29) | data formatting | bytes 2097152 | tf_op jit(solution)/shard_map/transpose | solution.py:507
  2.0 1.3 %fusion.8 = (bf16[8,4,64,128]{3,2,1,0:T(8,128)(2,1)}, bf16[8,4,64,128]{3,2,1,0:T(8,128)(2,1)}) fusion(bf16[8,4,64,256]{3,2,1,0:T(8,128)(2,1)S(1)} %bitcast.26), kind=kLoop, calls=%fused_computation.26 | loop fusion | bytes 2097152 | tf_op jit(solution)/shard_map/slice | solution.py:508
  3.3 0.0 copy-done.1
  3.3 0.4 slice_bitcast_fusion.1
  3.6 1.8 %copy.25 = bf16[32,192,128]{2,1,0:T(8,128)(2,1)} copy(bf16[32,192,128]{2,0,1:T(8,128)(2,1)S(1)} %slice_bitcast_fusion.1) | data formatting | bytes 3145728 | tf_op jit(solution)/shard_map/transpose | solution.py:503
  5.4 0.4 slice_bitcast_fusion
  5.7 0.3 fusion.7
  6.0 0.0 copy-start.3
  6.0 0.0 copy-start.2
  6.0 0.0 copy-start.4
  6.1 0.0 copy-start.5
  6.1 0.4 pad_maximum_fusion
  6.5 1.2 copy.26
  7.7 0.0 copy-start.6
  7.7 0.0 copy-done.3
  7.7 0.0 copy-done.2
  7.7 0.0 copy-done.4
  7.7 0.6 fusion.5.pack
  8.4 0.0 copy-done.5
  8.4 0.6 fusion.9
  10.8 0.0 copy-done
  10.9 0.9 copy.27
  11.8 1.0 constant_dynamic-slice_fusion.2
  12.8 0.7 copy.36
  15.4 0.8 constant_dynamic-slice_fusion.1
  16.3 0.8 copy.29
  17.0 1.0 constant_dynamic-slice_fusion
  18.1 0.7 copy.35
  18.7 0.0 copy-done.6
  18.7 0.1 broadcast_in_dim.10
  18.8 0.1 reshape.142
  19.0 0.1 reshape.143
  19.1 0.2 fusion.6
  19.3 0.7 pad_maximum_fusion.1
  20.0 0.8 tile.21.limit
  20.8 0.1 eq.19
  20.9 0.1 and_convert_fusion
  21.0 0.6 tile.19
  21.6 101.0 %fused.1 = bf16[16,896]{1,0:T(8,128)(2,1)} custom-call(bf16[8,4,64,128]{3,2,1,0:T(8,128)(2,1)} %get-tuple-element.8.key, bf16[8,4,192,128]{3,2,1,0:T(8,128)(2,1)} %bitcast.25, bf16[8,4,96,128]{3,2,1,0:T(8,128)(2,1)} %bitcast.27, f32[8,2176]{1,0:T(8,128)} %fusion.5.pack, bf16[8,4,64,128]{3,2,1,0:T(8,128)(2,1)} %get-tuple-element.7.val, ...), custom_call_target="tpu_custom_call" | custom-call | tf_op jit(solution)/shard_map/fused/pallas_call | solution.py:552
  122.6 0.8 reshape.147
  123.4 0.6 reshape.148
  (11 shorter events, 0.1 us)
Async XLA Ops:
  0.0 10.8 %copy-start = (bf16[8,1536,64]{1,2,0:T(8,128)(2,1)S(1)}, bf16[8,1536,64]{1,2,0:T(8,128)(2,1)}, u32[]{:S(2)}) copy-start(bf16[8,1536,64]{1,2,0:T(8,128)(2,1)} %param.21) | copy-start | bytes 4718596
  0.0 3.3 %copy-start.1 = (bf16[192,32,192]{2,1,0:T(8,128)(2,1)S(1)}, bf16[192,32,192]{2,1,0:T(8,128)(2,1)}, u32[]{:S(2)}) copy-start(bf16[192,32,192]{2,1,0:T(8,128)(2,1)} %param.19) | copy-start | bytes 7077892
  6.0 1.7 %copy-start.3 = (bf16[4,2,512]{2,1,0:T(2,128)(2,1)S(1)}, bf16[4,2,512]{2,1,0:T(2,128)(2,1)}, u32[]{:S(2)}) copy-start(bf16[4,2,512]{2,1,0:T(2,128)(2,1)} %param.15) | copy-start | bytes 24580
  6.0 1.7 %copy-start.2 = (bf16[4,2,1536]{2,1,0:T(2,128)(2,1)S(1)}, bf16[4,2,1536]{2,1,0:T(2,128)(2,1)}, u32[]{:S(2)}) copy-start(bf16[4,2,1536]{2,1,0:T(2,128)(2,1)} %param.14) | copy-start | bytes 73732
  6.0 1.7 %copy-start.4 = (bf16[4,2,64]{2,1,0:T(2,128)(2,1)S(1)}, bf16[4,2,64]{2,1,0:T(2,128)(2,1)}, u32[]{:S(2)}) copy-start(bf16[4,2,64]{2,1,0:T(2,128)(2,1)} %param.16) | copy-start | bytes 3076
  6.1 2.3 %copy-start.5 = (s32[2]{0:T(128)S(1)}, s32[2]{0:T(128)}, u32[]{:S(2)}) copy-start(s32[2]{0:T(128)} %param.18) | copy-start | bytes 28
  7.7 11.1 %copy-start.6 = (s32[16]{0:T(128)S(1)}, s32[16]{0:T(128)}, u32[]{:S(2)}) copy-start(s32[16]{0:T(128)} %param.17) | copy-start | bytes 196
